TPU v7x, 128 devices: a whole 4x4x4 slice. The times are simulated.
128 devices in a mesh: grp: 8 (over x, y_lo), sub: 16 (over y_hi, z, core).
Axes of the slice: x: 4, y: 4 (y_hi: 2, y_lo: 2; y = y_hi * 2 + y_lo), z: 4, core: 2. Of those that a mesh axis runs over, the one named last changes fastest.
Arguments:
- h1: bfloat16 [1048576, 256], P(('grp', 'sub')), may hold values from -6 to 6
- h2: bfloat16 [262144, 256], P(('grp', 'sub')), may hold values from -6 to 6
- nbr1: int32 [1048576, 8], P(('grp', 'sub')), may hold values from -1024 to 1024, as said below
- mask1: int32 [1048576, 8], P(('grp', 'sub')), may hold values 0 or 1
- owner: int32 [1048576], P(('grp', 'sub')), may hold values from 0 to 262143, as said below
- nbr2: int32 [262144, 8], P(('grp', 'sub')), may hold values from 0 to 262143, as said below
- mask2: int32 [262144, 8], P(('grp', 'sub')), may hold values 0 or 1
- a1: bfloat16 [256, 256], replicated, may hold values from -0.375 to 0.375
- b1: bfloat16 [256, 256], replicated, may hold values from -0.375 to 0.375
- m1: bfloat16 [256, 256], replicated, may hold values from -0.375 to 0.375
- u1: bfloat16 [256, 256], replicated, may hold values from -0.125 to 0.125
- a_up: bfloat16 [256, 256], replicated, may hold values from -0.375 to 0.375
- m_up: bfloat16 [256, 256], replicated, may hold values from -0.375 to 0.375
- u2: bfloat16 [256, 256], replicated, may hold values from -0.1875 to 0.1875
- a2: bfloat16 [256, 256], replicated, may hold values from -0.375 to 0.375
- b2: bfloat16 [256, 256], replicated, may hold values from -0.375 to 0.375
- m2: bfloat16 [256, 256], replicated, may hold values from -0.375 to 0.375
- v2: bfloat16 [256, 256], replicated, may hold values from -0.125 to 0.125
- a_down: bfloat16 [256, 256], replicated, may hold values from -0.375 to 0.375
- b_down: bfloat16 [256, 256], replicated, may hold values from -0.375 to 0.375
- m_down: bfloat16 [256, 256], replicated, may hold values from -0.375 to 0.375
Outputs:
- h1_out: bfloat16 [1048576, 256], P(('grp', 'sub'))
- h2_out: bfloat16 [262144, 256], P(('grp', 'sub'))
Inputs may be any that keep to these rules, and one draw needn't show every extreme that they name: i + nbr1[i, k] lies in 0 to 1048575; column 0 is max(-1024, -i) and column 7 is min(1024, 1048575 - i). owner[r] lies within 256 of r // 4 and in the same aligned block of 32768 rows as r // 4; the first of each device's 8192 rows points 256 below r // 4 and the last 256 above, where that block allows. nbr2[n, k] lies within 256 of n and in the same aligned block of 32768 rows as n; column 0 and column 7 reach 256 below and above where that block allows.
All inputs are finite; a program needn't handle non-finite values. No bound on the sum of `mask1` or of `mask2` on one device may be relied on, other than what follows from the above.
Results may differ from a plain program's by a relative error of at most 0.015.
Values may be sent and summed in bfloat16 or wider, within the bound.
No kernel may reach another device: no remote copies, remote signals or barrier semaphores. Data moves between devices by JAX's collectives and lax.ppermute only.
A program may use at most 128 MiB of HBM per device.

v0:
```python
import functools

import jax
import jax.numpy as jnp
from jax import lax
from jax.experimental import pallas as pl
from jax.experimental.pallas import tpu as pltpu
from jax.sharding import PartitionSpec as P

F32 = jnp.float32
BF16 = jnp.bfloat16
W = 256
L = 128
K = 8
C = 128
UNROLL = 4
HALF = 2
PIECE = 32
DEAD = -10000.0
EPS = 1e-05
VMEM_BYTES = 56 * 2**20
REACH1 = 1024
REACH2 = 256


def mm(x, y):
    return jnp.dot(x, y, preferred_element_type=F32)


def half(ref):
    return (ref[...].astype(F32) * 0.5).astype(BF16)


def centered(ref):
    w = ref[...].astype(F32)
    return (w - jnp.mean(w, axis=1, keepdims=True)).astype(BF16)


def act_of(y):
    return y + y * jnp.tanh(y)


def ones_block():
    return jnp.full((L, L), 1.0 / W, BF16)


def scale_of(y):
    lo = y[:, :L]
    hi = y[:, L:]
    s = jnp.sum(lo * lo + hi * hi, axis=1, keepdims=True)
    return lax.rsqrt(s * (1.0 / W) + EPS)


def store_table(tab, row0, p):
    n = p.shape[0]
    tab[pl.ds(2 * row0, n, stride=2), :] = p[:, :L]
    tab[pl.ds(2 * row0 + 1, n, stride=2), :] = p[:, L:]


def build_table(tab, ext, a, rows):
    step = 1024 if rows % 1024 == 0 else 512

    def one(b, carry):
        r = pl.multiple_of(b * step, step)
        store_table(tab, r, mm(ext[pl.ds(r, step), :], a))
        return carry

    lax.fori_loop(0, rows // step, one, 0)
    tab[pl.ds(2 * rows, 8), :] = jnp.full((8, L), DEAD, F32)


def build_dst(dst, ext, at, b, rows):
    step = 1024

    def one(i, carry):
        r = pl.multiple_of(i * step, step)
        dst[pl.ds(r, step), :] = mm(ext[pl.ds(at + r, step), :], b)
        return carry

    lax.fori_loop(0, rows // step, one, 0)


def edge_loop(nc, idx_vm, slots, sems, bufs, tab, dst, mc, z, post, finish):
    def fetch(c, s):
        return pltpu.make_async_copy(idx_vm.at[jnp.minimum(c, nc - 1)], slots[s], sems.at[s])

    def gather(slot, buf, k):
        for i in range(C):
            j = slot[k, i]
            buf[pl.ds(2 * (k * C + i), 2), :] = tab[pl.ds(j, 2), :]

    def piece(buf, node, i0, zrow):
        d = dst[pl.ds(node + i0, PIECE), :]
        d0 = d[:, :L]
        d1 = d[:, L:]
        acts = []
        for k in range(K):
            base = 2 * (k * C + i0)
            y0 = buf[pl.ds(base, PIECE, stride=2), :] + d0
            y1 = buf[pl.ds(base + 1, PIECE, stride=2), :] + d1
            acts.append(jnp.concatenate([act_of(y0), act_of(y1)], axis=1).astype(BF16))
        w = scale_of(mm(jnp.concatenate(acts, axis=0), mc[...]))
        acc0 = acc1 = None
        for k in range(K):
            wk = w[k * PIECE : (k + 1) * PIECE]
            a = acts[k].astype(F32)
            t0 = a[:, :L] * wk
            t1 = a[:, L:] * wk
            acc0 = t0 if k == 0 else acc0 + t0
            acc1 = t1 if k == 0 else acc1 + t1
        z[pl.ds(zrow + i0, PIECE), :] = jnp.concatenate([acc0, acc1], axis=1).astype(BF16)

    z[...] = jnp.zeros(z.shape, BF16)
    for s in range(UNROLL):
        fetch(s, s).start()
    fetch(0, 0).wait()
    for k in range(K):
        gather(slots[0], bufs[0], k)
    fetch(UNROLL, 0).start()

    def body(t, carry):
        for g in range(UNROLL):
            c = t * UNROLL + g
            nxt = (g + 1) % UNROLL
            node = pl.multiple_of(c * C, C)
            if g % HALF == 0:
                for s in range(HALF):
                    fetch(c + 1 + s, (nxt + s) % UNROLL).wait()
                part = g // HALF
                pair = t * (UNROLL // HALF) + part
                post(pair - 1, 1 - part)
                finish(pair - 2, part)
            for p in range(C // PIECE):
                for k in range(p * PIECE * K // C, (p + 1) * PIECE * K // C):
                    gather(slots[nxt], bufs[(g + 1) % 2], k)
                piece(bufs[g % 2], node, p * PIECE, g * C)
            if g % HALF == HALF - 1:
                for s in range(HALF):
                    n = c + 1 + UNROLL - HALF + 1 + s
                    fetch(n, (nxt - HALF + 1 + s) % UNROLL).start()
        return carry

    lax.fori_loop(0, nc // UNROLL, body, 0)
    pairs = nc // HALF
    post(pairs - 1, 1)
    finish(pairs - 2, 0)
    finish(pairs - 1, 1)
    for s in range(UNROLL):
        fetch(0, s).wait()


PAIR = HALF * C


def level1_kernel(
    base_ref, nbr, mask, owner, h1, prev, nxt, a1, b1, m1, u1, a_up, m_up, h1a, part, send_lo, send_hi,
    ext, tab, dst, idx_vm, s0, s1, s2, s3, r0, r1, z, msg, mc, mu, ma, mupc, fsem, csem
):
    nodes = h1a.shape[0]
    rows = ext.shape[0]
    loads = [(h1, REACH1, nodes), (prev, 0, REACH1), (nxt, REACH1 + nodes, REACH1)]
    copies = [
        pltpu.make_async_copy(src, ext.at[pl.ds(at, n), :], csem.at[i])
        for i, (src, at, n) in enumerate(loads)
    ]
    for cp in copies:
        cp.start()

    lane = lax.broadcasted_iota(jnp.int32, (K, L), 1)
    for c in range(nodes // C):
        cols = slice(c * C, (c + 1) * C)
        row = nbr[:, cols] + (lane + (REACH1 + c * C))
        idx_vm[c] = 2 * jnp.where(mask[:, cols] > 0, row, rows)
    mcv = centered(m1)
    mc[...] = mcv
    mu[...] = mm(mcv, u1[...]).astype(BF16)
    ma[...] = half(a_up)
    mupc[...] = centered(m_up)
    part[...] = jnp.zeros(part.shape, F32)
    msg[...] = jnp.zeros(msg.shape, BF16)
    for cp in copies:
        cp.wait()
    build_table(tab, ext, half(a1), rows)
    build_dst(dst, ext, REACH1, half(b1), nodes)

    def post(step, at):
        node = pl.multiple_of(jnp.maximum(step, 0) * PAIR, PAIR)
        hrow = ext[pl.ds(node + REACH1, PAIR), :].astype(F32)
        hb = (hrow + mm(z[pl.ds(at * PAIR, PAIR), :], mu[...])).astype(BF16)
        h1a[pl.ds(node, PAIR), :] = hb
        y = mm(act_of(mm(hb, ma[...])).astype(BF16), mupc[...])
        w = scale_of(y)
        msg[pl.ds(at * PAIR, PAIR), :] = jnp.concatenate(
            [y[:, :L] * w, y[:, L:] * w], axis=1
        ).astype(BF16)

    win = PAIR // 4 + 2 * REACH2

    def finish(step, at):
        live = jnp.where(step >= 0, 1.0, 0.0).astype(F32)
        pair = jnp.maximum(step, 0)
        first = pair * (PAIR // 4)
        ids = lax.broadcasted_iota(jnp.int32, (win, L), 0) + (base_ref[0] + first - REACH2)
        hot = []
        for j in range(HALF):
            ow = owner[pl.ds(pair * HALF + j, 1), :]
            hot.append(jnp.where(ids == ow, live, 0.0).astype(BF16))
        spot = pl.multiple_of(first, PAIR // 4)
        part[pl.ds(spot, win), :] += mm(
            jnp.concatenate(hot, axis=1), msg[pl.ds(at * PAIR, PAIR), :]
        )

    edge_loop(
        nodes // C, idx_vm, (s0, s1, s2, s3), fsem, (r0, r1), tab, dst, mc, z, post, finish
    )
    n = 2 * REACH2
    send_lo[...] = part[pl.ds(0, n), :].astype(BF16)
    send_hi[...] = part[pl.ds(part.shape[0] - n, n), :].astype(BF16)


def vmem():
    return pl.BlockSpec(memory_space=pltpu.VMEM)


def anyspace():
    return pl.BlockSpec(memory_space=pl.ANY)


def gather_scratch(rows, nodes):
    return [
        pltpu.VMEM((2 * rows + 8, L), F32),
        pltpu.VMEM((nodes, W), F32),
        pltpu.VMEM((nodes // C, K, L), jnp.int32),
        *[pltpu.SMEM((K, L), jnp.int32) for _ in range(UNROLL)],
        *[pltpu.VMEM((2 * K * C, L), F32) for _ in range(2)],
        pltpu.VMEM((UNROLL * C, W), BF16),
    ]


def level1(base, nbr_t, mask_t, owner2, h1, prev, nxt, weights):
    nodes = h1.shape[0]
    rows = nodes + 2 * REACH1
    n2 = nodes // 4
    edges = nodes * K
    shape = jax.ShapeDtypeStruct
    return pl.pallas_call(
        level1_kernel,
        out_shape=[
            shape((nodes, W), BF16),
            shape((n2 + 2 * REACH2, W), F32),
            shape((2 * REACH2, W), BF16),
            shape((2 * REACH2, W), BF16),
        ],
        in_specs=[pl.BlockSpec(memory_space=pltpu.SMEM)]
        + [vmem()] * 3
        + [anyspace()] * 3
        + [vmem()] * len(weights),
        out_specs=[vmem()] * 4,
        scratch_shapes=[
            pltpu.VMEM((rows, W), BF16),
            *gather_scratch(rows, nodes),
            pltpu.VMEM((UNROLL * C, W), BF16),
            *[pltpu.VMEM((W, W), BF16) for _ in range(4)],
            pltpu.SemaphoreType.DMA((UNROLL,)),
            pltpu.SemaphoreType.DMA((3,)),
        ],
        compiler_params=pltpu.CompilerParams(vmem_limit_bytes=VMEM_BYTES),
        cost_estimate=pl.CostEstimate(
            flops=4 * edges * W * W, bytes_accessed=rows * W * 4, transcendentals=edges * W
        ),
        name="level1",
    )(base, nbr_t, mask_t, owner2, h1, prev, nxt, *weights)


def level2_kernel(
    base_ref, nbr, mask, part, from_lo, from_hi, h2, lo2, hi2, u2, a2, b2, m2, v2, h2o, edge_lo, edge_hi,
    h2x, tab, dst, idx_vm, s0, s1, s2, s3, r0, r1, z, mc, mv, fsem
):
    n2 = h2o.shape[0]
    rows = n2 + 2 * REACH2
    S = 2 * REACH2
    u = u2[...]
    for q in range(rows // S):
        piece = part[pl.ds(q * S, S), :]
        if q == 0:
            piece = piece + from_lo[...].astype(F32)
        elif q == rows // S - 1:
            piece = piece + from_hi[...].astype(F32)
        d = mm(piece.astype(BF16), u)
        for hf in range(2):
            at = q * S + hf * REACH2
            if at == 0:
                src = lo2[...]
            elif at == rows - REACH2:
                src = hi2[...]
            else:
                src = h2[pl.ds(at - REACH2, REACH2), :]
            dd = d[hf * REACH2 : (hf + 1) * REACH2]
            h2x[pl.ds(at, REACH2), :] = (src.astype(F32) + dd).astype(BF16)
    lane = lax.broadcasted_iota(jnp.int32, (K, L), 1)
    base = base_ref[0]
    for c in range(n2 // C):
        cols = slice(c * C, (c + 1) * C)
        row = nbr[:, cols] - (base - REACH2)
        idx_vm[c] = 2 * jnp.where(mask[:, cols] > 0, row, rows)
    mcv = centered(m2)
    mc[...] = mcv
    mv[...] = mm(mcv, v2[...]).astype(BF16)
    build_table(tab, h2x, half(a2), rows)
    build_dst(dst, h2x, REACH2, half(b2), n2)

    def post(step, at):
        node = pl.multiple_of(jnp.maximum(step, 0) * PAIR, PAIR)
        hrow = h2x[pl.ds(node + REACH2, PAIR), :].astype(F32)
        h2o[pl.ds(node, PAIR), :] = (hrow + mm(z[pl.ds(at * PAIR, PAIR), :], mv[...])).astype(BF16)

    edge_loop(
        n2 // C, idx_vm, (s0, s1, s2, s3), fsem, (r0, r1), tab, dst, mc, z, post, lambda p, at: None
    )
    edge_lo[...] = h2o[pl.ds(0, REACH2), :]
    edge_hi[...] = h2o[pl.ds(n2 - REACH2, REACH2), :]


def level2(base, nbr_t, mask_t, part, from_lo, from_hi, h2, lo2, hi2, weights):
    nodes = h2.shape[0]
    rows = nodes + 2 * REACH2
    args = (base, nbr_t, mask_t, part, from_lo, from_hi, h2, lo2, hi2, *weights)
    shape = jax.ShapeDtypeStruct
    return pl.pallas_call(
        level2_kernel,
        out_shape=[shape((nodes, W), BF16), shape((REACH2, W), BF16), shape((REACH2, W), BF16)],
        in_specs=[pl.BlockSpec(memory_space=pltpu.SMEM)] + [vmem()] * (len(args) - 1),
        out_specs=[vmem()] * 3,
        scratch_shapes=[
            pltpu.VMEM((rows, W), BF16),
            *gather_scratch(rows, nodes),
            pltpu.VMEM((W, W), BF16),
            pltpu.VMEM((W, W), BF16),
            pltpu.SemaphoreType.DMA((UNROLL,)),
        ],
        compiler_params=pltpu.CompilerParams(vmem_limit_bytes=VMEM_BYTES),
        cost_estimate=pl.CostEstimate(
            flops=4 * nodes * K * W * W, bytes_accessed=rows * W * 4, transcendentals=nodes * K * W
        ),
        name="level2",
    )(*args)


DOWN = 2048
GROUP = 512


def down_kernel(base_ref, owner, h1a, h2o, lo, hi, a_down, b_down, m_down, o_ref, pd, bd, mdc):
    t = pl.program_id(0)
    n2 = h2o.shape[0]

    @pl.when(t == 0)
    def _():
        a = half(a_down)
        pd[pl.ds(0, REACH2), :] = mm(lo[...], a).astype(BF16)
        for b in range(n2 // 256):
            pd[pl.ds(REACH2 + b * 256, 256), :] = mm(h2o[pl.ds(b * 256, 256), :], a).astype(BF16)
        pd[pl.ds(REACH2 + n2, REACH2), :] = mm(hi[...], a).astype(BF16)
        bd[...] = half(b_down)
        mdc[...] = centered(m_down)

    win = GROUP // 4 + 2 * REACH2
    lane = lax.broadcasted_iota(jnp.int32, (L, L), 1).astype(F32)
    for g in range(DOWN // GROUP):
        start = t * (DOWN // 4) + g * (GROUP // 4)
        lowest = base_ref[0] + start - REACH2
        table = pd[pl.ds(pl.multiple_of(start, L), win), :]
        hot = []
        for j in range(GROUP // L):
            ow = owner[pl.ds(t * (DOWN // L) + g * (GROUP // L) + j, 1), :] - lowest
            col = jnp.transpose(jnp.broadcast_to(ow.astype(F32), (L, L)))
            hot.append(
                jnp.concatenate(
                    [jnp.where(col == lane + q * L, 1.0, 0.0).astype(BF16) for q in range(win // L)],
                    axis=1,
                )
            )
        hb = h1a[pl.ds(g * GROUP, GROUP), :]
        y = mm(jnp.concatenate(hot, axis=0), table) + mm(hb, bd[...])
        d = mm(act_of(y).astype(BF16), mdc[...])
        w = scale_of(d)
        ln = jnp.concatenate([d[:, :L] * w, d[:, L:] * w], axis=1)
        o_ref[pl.ds(g * GROUP, GROUP), :] = (hb.astype(F32) + ln).astype(BF16)


def down(base, owner2, h1a, h2o, lo, hi, a_down, b_down, m_down):
    nodes1 = h1a.shape[0]
    n2 = h2o.shape[0]

    def whole(shape):
        return pl.BlockSpec(shape, lambda t: (0, 0))

    block = pl.BlockSpec((DOWN, W), lambda t: (t, 0))
    return pl.pallas_call(
        down_kernel,
        grid=(nodes1 // DOWN,),
        out_shape=jax.ShapeDtypeStruct((nodes1, W), BF16),
        in_specs=[
            pl.BlockSpec(memory_space=pltpu.SMEM),
            whole(owner2.shape),
            block,
            whole((n2, W)),
            whole((REACH2, W)),
            whole((REACH2, W)),
            whole((W, W)),
            whole((W, W)),
            whole((W, W)),
        ],
        out_specs=block,
        scratch_shapes=[
            pltpu.VMEM((n2 + 2 * REACH2, W), BF16),
            pltpu.VMEM((W, W), BF16),
            pltpu.VMEM((W, W), BF16),
        ],
        compiler_params=pltpu.CompilerParams(vmem_limit_bytes=VMEM_BYTES),
        cost_estimate=pl.CostEstimate(
            flops=10 * nodes1 * W * W, bytes_accessed=nodes1 * W * 4, transcendentals=nodes1 * W
        ),
        name="down",
    )(base, owner2, h1a, h2o, lo, hi, a_down, b_down, m_down)


def swap(to_next, to_prev, axis):
    count = lax.axis_size(axis)
    ends = count - 1
    from_prev = lax.ppermute(to_next, axis, [(i, (i + 1) % count) for i in range(ends)])
    from_next = lax.ppermute(to_prev, axis, [((i + 1) % count, i) for i in range(ends)])
    return from_prev, from_next


def shards(
    h1,
    h2,
    nbr1,
    mask1,
    owner,
    nbr2,
    mask2,
    a1,
    b1,
    m1,
    u1,
    a_up,
    m_up,
    u2,
    a2,
    b2,
    m2,
    v2,
    a_down,
    b_down,
    m_down,
):
    nodes1 = h1.shape[0]
    nodes2 = h2.shape[0]
    device = lax.axis_index("grp") * lax.axis_size("sub") + lax.axis_index("sub")
    base = jnp.reshape(device * nodes2, (1,)).astype(jnp.int32)
    nbr1_t, mask1_t, nbr2_t, mask2_t = nbr1.T, mask1.T, nbr2.T, mask2.T
    owner2 = owner.reshape(nodes1 // L, L)
    halo1 = swap(h1[nodes1 - REACH1 :], h1[:REACH1], ("grp", "sub"))
    halo2 = swap(h2[nodes2 - REACH2 :], h2[:REACH2], "sub")
    h1a, part, send_lo, send_hi = level1(
        base, nbr1_t, mask1_t, owner2, h1, *halo1, (a1, b1, m1, u1, a_up, m_up)
    )
    from_lo, from_hi = swap(send_hi, send_lo, "sub")
    h2_out, edge_lo, edge_hi = level2(
        base, nbr2_t, mask2_t, part, from_lo, from_hi, h2, *halo2, (u2, a2, b2, m2, v2)
    )
    lo, hi = swap(edge_hi, edge_lo, "sub")
    h1_out = down(base, owner2, h1a, h2_out, lo, hi, a_down, b_down, m_down)
    return (h1_out, h2_out)


def solution(mesh):
    split = P(("grp", "sub"), None)
    return jax.shard_map(
        shards,
        mesh=mesh,
        in_specs=(split, split, split, split, P(("grp", "sub")), split, split) + (P(),) * 14,
        out_specs=(split, split),
        check_vma=False,
    )
```

profile of v0, /device:TPU:103, one launch (start us, length us, event | category | flops | bytes accessed | tf_op | source)
XLA Modules:
  0.0 181.5 jit_solution(5238436729105147026)
XLA Ops:
  0.6 1.3 fusion
  1.9 2.6 %collective-permute-start.1 = (bf16[1024,256]{1,0:T(8,128)(2,1)S(1)}, bf16[1024,256]{1,0:T(8,128)(2,1)S(1)}, u32[]{:S(2)}, u32[]{:S(2)}) collective-permute-start(bf16[1024,256]{1,0:T(8,128)(2,1)S(1)} %get-tuple-element.16), channel_id=1, source_target_pairs={{1,0},{2,1},{3,2},{4,3},{5,4},{6,5},{7,6},{8,7},{9,8},{10,9},{11,1... | collective-permute-start | bytes 1572872 | tf_op jit(solution)/shard_map/ppermute | solution.py:432
  4.5 6.6 %collective-permute-start = (bf16[1024,256]{1,0:T(8,128)(2,1)S(1)}, bf16[1024,256]{1,0:T(8,128)(2,1)S(1)}, u32[]{:S(2)}, u32[]{:S(2)}) collective-permute-start(bf16[1024,256]{1,0:T(8,128)(2,1)S(1)} %get-tuple-element.17), channel_id=1, source_target_pairs={{0,1},{1,2},{2,3},{3,4},{4,5},{5,6},{6,7},{7,8},{8,9},{9,10},{10,1... | collective-permute-start | bytes 1572872 | tf_op jit(solution)/shard_map/ppermute | solution.py:431
  11.1 4.9 %collective-permute-done.1.nxt = bf16[1024,256]{1,0:T(8,128)(2,1)S(1)} collective-permute-done((bf16[1024,256]{1,0:T(8,128)(2,1)S(1)}, bf16[1024,256]{1,0:T(8,128)(2,1)S(1)}, u32[]{:S(2)}, u32[]{:S(2)}) %collective-permute-start.1) | collective-permute-done | bytes 524320 | tf_op jit(solution)/shard_map/ppermute | solution.py:432
  16.0 0.0 copy-start
  16.0 1.2 collective-permute-done.prev
  17.2 0.0 copy-start.1
  17.2 0.0 copy-done
  17.2 0.8 copy-done.1
  18.0 84.3 %level1.1 = (bf16[8192,256]{1,0:T(8,128)(2,1)}, f32[2560,256]{1,0:T(8,128)}, bf16[512,256]{1,0:T(8,128)(2,1)}, bf16[512,256]{1,0:T(8,128)(2,1)}) custom-call(s32[1]{0:T(128)} %bitcast.base_ref, s32[8,8192]{1,0:T(8,128)} %bitcast.6, s32[8,8192]{1,0:T(8,128)} %bitcast.7, s32[64,128]{1,0:T(8,128)} %bitcast.10, bf16[8192,256]{1,0:T(8,128)(2,1)} %h1.1, ...), custom_call_target="tpu_custom_call" | custom-call | flops 17179869184 | bytes 10485760 | tf_op jit(solution)/shard_map/level1/pallas_call | solution.py:246
  102.3 8.1 %collective-permute-start.2 = (bf16[512,256]{1,0:T(8,128)(2,1)}, bf16[512,256]{1,0:T(8,128)(2,1)S(1)}, u32[]{:S(2)}, u32[]{:S(2)}) collective-permute-start(bf16[512,256]{1,0:T(8,128)(2,1)} %get-tuple-element.11), channel_id=1, source_target_pairs={{0,1},{1,2},{2,3},{3,4},{4,5},{5,6},{6,7},{7,8},{8,9},{9,10},{10,1... | collective-permute-start | bytes 786440 | tf_op jit(solution)/shard_map/ppermute | solution.py:431
  110.4 1.9 %collective-permute-start.3 = (bf16[512,256]{1,0:T(8,128)(2,1)}, bf16[512,256]{1,0:T(8,128)(2,1)S(1)}, u32[]{:S(2)}, u32[]{:S(2)}) collective-permute-start(bf16[512,256]{1,0:T(8,128)(2,1)} %get-tuple-element.12), channel_id=1, source_target_pairs={{1,0},{2,1},{3,2},{4,3},{5,4},{6,5},{7,6},{8,7},{9,8},{10,9},{11,1... | collective-permute-start | bytes 786440 | tf_op jit(solution)/shard_map/ppermute | solution.py:432
  112.4 1.0 fusion.1
  113.3 1.9 %collective-permute-start.5 = (bf16[256,256]{1,0:T(8,128)(2,1)S(1)}, bf16[256,256]{1,0:T(8,128)(2,1)S(1)}, u32[]{:S(2)}, u32[]{:S(2)}) collective-permute-start(bf16[256,256]{1,0:T(8,128)(2,1)S(1)} %get-tuple-element.18), channel_id=1, source_target_pairs={{1,0},{2,1},{3,2},{4,3},{5,4},{6,5},{7,6},{8,7},{9,8},{10,9},{11,1... | collective-permute-start | bytes 393224 | tf_op jit(solution)/shard_map/ppermute | solution.py:432
  115.3 7.3 %collective-permute-start.4 = (bf16[256,256]{1,0:T(8,128)(2,1)S(1)}, bf16[256,256]{1,0:T(8,128)(2,1)S(1)}, u32[]{:S(2)}, u32[]{:S(2)}) collective-permute-start(bf16[256,256]{1,0:T(8,128)(2,1)S(1)} %get-tuple-element.19), channel_id=1, source_target_pairs={{0,1},{1,2},{2,3},{3,4},{4,5},{5,6},{6,7},{7,8},{8,9},{9,10},{10,1... | collective-permute-start | bytes 393224 | tf_op jit(solution)/shard_map/ppermute | solution.py:431
  122.5 0.8 collective-permute-done.5.hi2
  123.3 0.0 copy-start.4
  123.3 1.1 collective-permute-done.4.lo2
  124.5 0.0 copy-start.5
  124.5 0.0 collective-permute-done.2.from_lo
  124.5 0.0 copy-start.2
  124.5 0.0 collective-permute-done.3.from_hi
  124.5 0.0 copy-start.3
  124.5 0.0 copy-done.4
  124.5 0.6 copy-done.5
  125.1 0.1 copy-done.2
  125.2 0.1 copy-done.3
  125.3 22.5 %level2.1 = (bf16[2048,256]{1,0:T(8,128)(2,1)}, bf16[256,256]{1,0:T(8,128)(2,1)}, bf16[256,256]{1,0:T(8,128)(2,1)}) custom-call(s32[1]{0:T(128)} %bitcast.base_ref, s32[8,2048]{1,0:T(8,128)} %bitcast.8, s32[8,2048]{1,0:T(8,128)} %bitcast.9, f32[2560,256]{1,0:T(8,128)} %get-tuple-element.10.part, bf16[512,256]{1,0:T(8,128)(2,1)} %copy-done.2, ...), custom_call_target="tpu_custom_call" | custom-call | flops 4294967296 | bytes 2621440 | tf_op jit(solution)/shard_map/level2/pallas_call | solution.py:329
  147.8 8.0 %collective-permute-start.6 = (bf16[256,256]{1,0:T(8,128)(2,1)}, bf16[256,256]{1,0:T(8,128)(2,1)S(1)}, u32[]{:S(2)}, u32[]{:S(2)}) collective-permute-start(bf16[256,256]{1,0:T(8,128)(2,1)} %get-tuple-element.14), channel_id=1, source_target_pairs={{0,1},{1,2},{2,3},{3,4},{4,5},{5,6},{6,7},{7,8},{8,9},{9,10},{10,1... | collective-permute-start | bytes 393224 | tf_op jit(solution)/shard_map/ppermute | solution.py:431
  155.8 2.1 %collective-permute-start.7 = (bf16[256,256]{1,0:T(8,128)(2,1)}, bf16[256,256]{1,0:T(8,128)(2,1)S(1)}, u32[]{:S(2)}, u32[]{:S(2)}) collective-permute-start(bf16[256,256]{1,0:T(8,128)(2,1)} %get-tuple-element.15), channel_id=1, source_target_pairs={{1,0},{2,1},{3,2},{4,3},{5,4},{6,5},{7,6},{8,7},{9,8},{10,9},{11,1... | collective-permute-start | bytes 393224 | tf_op jit(solution)/shard_map/ppermute | solution.py:432
  157.9 0.1 collective-permute-done.6.lo
  158.0 0.0 copy-start.6
  158.0 7.9 %collective-permute-done.7.hi = bf16[256,256]{1,0:T(8,128)(2,1)S(1)} collective-permute-done((bf16[256,256]{1,0:T(8,128)(2,1)}, bf16[256,256]{1,0:T(8,128)(2,1)S(1)}, u32[]{:S(2)}, u32[]{:S(2)}) %collective-permute-start.7) | collective-permute-done | bytes 131104 | tf_op jit(solution)/shard_map/ppermute | solution.py:432
  165.9 0.0 copy-start.7
  165.9 0.0 copy-done.6
  165.9 0.6 copy-done.7
  166.5 14.9 %down.1 = bf16[8192,256]{1,0:T(8,128)(2,1)} custom-call(s32[1]{0:T(128)} %bitcast.base_ref, s32[64,128]{1,0:T(8,128)} %bitcast.11, bf16[8192,256]{1,0:T(8,128)(2,1)} %get-tuple-element.9.h1a, bf16[2048,256]{1,0:T(8,128)(2,1)} %get-tuple-element.8.h2o, bf16[256,256]{1,0:T(8,128)(2,1)} %copy-done.6, bf16[256,256]{1,0:T(8,128)(2,1)} %copy-done.7, ...), custom_call_target="tpu_custom_call" | custom-call | flops 5368709120 | bytes 8388608 | tf_op jit(solution)/shard_map/down/pallas_call | solution.py:399
Async XLA Ops:
  1.9 14.1 %collective-permute-start.1 = (bf16[1024,256]{1,0:T(8,128)(2,1)S(1)}, bf16[1024,256]{1,0:T(8,128)(2,1)S(1)}, u32[]{:S(2)}, u32[]{:S(2)}) collective-permute-start(bf16[1024,256]{1,0:T(8,128)(2,1)S(1)} %get-tuple-element.16), channel_id=1, source_target_pairs={{1,0},{2,1},{3,2},{4,3},{5,4},{6,5},{7,6},{8,7},{9,8},{10,9},{11,1... | collective-permute-start | bytes 1572872 | tf_op jit(solution)/shard_map/ppermute | solution.py:432
  4.5 12.7 %collective-permute-start = (bf16[1024,256]{1,0:T(8,128)(2,1)S(1)}, bf16[1024,256]{1,0:T(8,128)(2,1)S(1)}, u32[]{:S(2)}, u32[]{:S(2)}) collective-permute-start(bf16[1024,256]{1,0:T(8,128)(2,1)S(1)} %get-tuple-element.17), channel_id=1, source_target_pairs={{0,1},{1,2},{2,3},{3,4},{4,5},{5,6},{6,7},{7,8},{8,9},{9,10},{10,1... | collective-permute-start | bytes 1572872 | tf_op jit(solution)/shard_map/ppermute | solution.py:431
  16.0 1.2 copy-start
  17.2 0.8 copy-start.1
  102.3 22.1 %collective-permute-start.2 = (bf16[512,256]{1,0:T(8,128)(2,1)}, bf16[512,256]{1,0:T(8,128)(2,1)S(1)}, u32[]{:S(2)}, u32[]{:S(2)}) collective-permute-start(bf16[512,256]{1,0:T(8,128)(2,1)} %get-tuple-element.11), channel_id=1, source_target_pairs={{0,1},{1,2},{2,3},{3,4},{4,5},{5,6},{6,7},{7,8},{8,9},{9,10},{10,1... | collective-permute-start | bytes 786440 | tf_op jit(solution)/shard_map/ppermute | solution.py:431
  110.4 14.0 %collective-permute-start.3 = (bf16[512,256]{1,0:T(8,128)(2,1)}, bf16[512,256]{1,0:T(8,128)(2,1)S(1)}, u32[]{:S(2)}, u32[]{:S(2)}) collective-permute-start(bf16[512,256]{1,0:T(8,128)(2,1)} %get-tuple-element.12), channel_id=1, source_target_pairs={{1,0},{2,1},{3,2},{4,3},{5,4},{6,5},{7,6},{8,7},{9,8},{10,9},{11,1... | collective-permute-start | bytes 786440 | tf_op jit(solution)/shard_map/ppermute | solution.py:432
  113.3 10.0 %collective-permute-start.5 = (bf16[256,256]{1,0:T(8,128)(2,1)S(1)}, bf16[256,256]{1,0:T(8,128)(2,1)S(1)}, u32[]{:S(2)}, u32[]{:S(2)}) collective-permute-start(bf16[256,256]{1,0:T(8,128)(2,1)S(1)} %get-tuple-element.18), channel_id=1, source_target_pairs={{1,0},{2,1},{3,2},{4,3},{5,4},{6,5},{7,6},{8,7},{9,8},{10,9},{11,1... | collective-permute-start | bytes 393224 | tf_op jit(solution)/shard_map/ppermute | solution.py:432
  115.3 9.2 %collective-permute-start.4 = (bf16[256,256]{1,0:T(8,128)(2,1)S(1)}, bf16[256,256]{1,0:T(8,128)(2,1)S(1)}, u32[]{:S(2)}, u32[]{:S(2)}) collective-permute-start(bf16[256,256]{1,0:T(8,128)(2,1)S(1)} %get-tuple-element.19), channel_id=1, source_target_pairs={{0,1},{1,2},{2,3},{3,4},{4,5},{5,6},{6,7},{7,8},{8,9},{9,10},{10,1... | collective-permute-start | bytes 393224 | tf_op jit(solution)/shard_map/ppermute | solution.py:431
  123.3 1.1 copy-start.4
  124.5 0.7 copy-start.5
  124.5 0.7 copy-start.2
  124.5 0.8 copy-start.3
  147.8 10.2 %collective-permute-start.6 = (bf16[256,256]{1,0:T(8,128)(2,1)}, bf16[256,256]{1,0:T(8,128)(2,1)S(1)}, u32[]{:S(2)}, u32[]{:S(2)}) collective-permute-start(bf16[256,256]{1,0:T(8,128)(2,1)} %get-tuple-element.14), channel_id=1, source_target_pairs={{0,1},{1,2},{2,3},{3,4},{4,5},{5,6},{6,7},{7,8},{8,9},{9,10},{10,1... | collective-permute-start | bytes 393224 | tf_op jit(solution)/shard_map/ppermute | solution.py:431
  155.8 10.1 %collective-permute-start.7 = (bf16[256,256]{1,0:T(8,128)(2,1)}, bf16[256,256]{1,0:T(8,128)(2,1)S(1)}, u32[]{:S(2)}, u32[]{:S(2)}) collective-permute-start(bf16[256,256]{1,0:T(8,128)(2,1)} %get-tuple-element.15), channel_id=1, source_target_pairs={{1,0},{2,1},{3,2},{4,3},{5,4},{6,5},{7,6},{8,7},{9,8},{10,9},{11,1... | collective-permute-start | bytes 393224 | tf_op jit(solution)/shard_map/ppermute | solution.py:432
  158.0 7.9 %copy-start.6 = (bf16[256,256]{1,0:T(8,128)(2,1)}, bf16[256,256]{1,0:T(8,128)(2,1)S(1)}, u32[]{:S(2)}) copy-start(bf16[256,256]{1,0:T(8,128)(2,1)S(1)} %collective-permute-done.6.lo) | copy-start | bytes 393220
  165.9 0.7 copy-start.7
where the time goes:
time: 182 us; the launch traced here: 181 us
  Pallas kernels  122 us (67%)
  starting transfers between devices  38.4 us (21%)
  waiting for transfers between devices  16 us (9%)
  local copies, waits for them, and re-layouts  4.51 us (2%)
    pallas_call x1, Pallas kernels, level1(): pl.pallas_call(level1_kernel, out_shape=[shape((nodes, W), BF16), shape((...  84.3 us
    ppermute x4, starting transfers between devices, swap(): lax.ppermute(to_next, axis, [(i, (i + 1) % count) for i in range(ends)])  29.9 us
    pallas_call x1, Pallas kernels, level2(): pl.pallas_call(level2_kernel, out_shape=[shape((nodes, W), BF16), shape((...  22.5 us
    pallas_call x1, Pallas kernels, down(): pl.pallas_call(down_kernel, grid=(nodes1 // DOWN,), out_shape=jax.ShapeDt...  14.9 us
    ppermute x4, waiting for transfers between devices, swap(): lax.ppermute(to_prev, axis, [((i + 1) % count, i) for i in range(ends)])  13.6 us
    ppermute x4, starting transfers between devices, swap(): lax.ppermute(to_prev, axis, [((i + 1) % count, i) for i in range(ends)])  8.52 us
  transfers between devices with their start and end apart: 8, of which 6 were waited for; matrix products, arithmetic and copies ran while one was open for 1% of the time, Pallas kernels for 0%

commit v1 on v0

--- a/solution.py
+++ b/solution.py
@@ -15,6 +15,7 @@
 C = 128
 UNROLL = 4
 HALF = 2
+PAIR = HALF * C
 PIECE = 32
 DEAD = -10000.0
 EPS = 1e-05
@@ -57,30 +58,18 @@
     tab[pl.ds(2 * row0 + 1, n, stride=2), :] = p[:, L:]
 
 
-def build_table(tab, ext, a, rows):
+def build_table(tab, ext, a, row0, rows):
     step = 1024 if rows % 1024 == 0 else 512
 
     def one(b, carry):
-        r = pl.multiple_of(b * step, step)
+        r = pl.multiple_of(row0 + b * step, step)
         store_table(tab, r, mm(ext[pl.ds(r, step), :], a))
         return carry
 
     lax.fori_loop(0, rows // step, one, 0)
-    tab[pl.ds(2 * rows, 8), :] = jnp.full((8, L), DEAD, F32)
-
-
-def build_dst(dst, ext, at, b, rows):
-    step = 1024
-
-    def one(i, carry):
-        r = pl.multiple_of(i * step, step)
-        dst[pl.ds(r, step), :] = mm(ext[pl.ds(at + r, step), :], b)
-        return carry
-
-    lax.fori_loop(0, rows // step, one, 0)
-
-
-def edge_loop(nc, idx_vm, slots, sems, bufs, tab, dst, mc, z, post, finish):
+
+
+def edge_loop(nc, idx_vm, slots, sems, bufs, tab, dst, mc, z, receivers, post, finish):
     def fetch(c, s):
         return pltpu.make_async_copy(idx_vm.at[jnp.minimum(c, nc - 1)], slots[s], sems.at[s])
 
@@ -89,8 +78,8 @@
             j = slot[k, i]
             buf[pl.ds(2 * (k * C + i), 2), :] = tab[pl.ds(j, 2), :]
 
-    def piece(buf, node, i0, zrow):
-        d = dst[pl.ds(node + i0, PIECE), :]
+    def piece(buf, i0, zrow):
+        d = dst[pl.ds(zrow + i0, PIECE), :]
         d0 = d[:, :L]
         d1 = d[:, L:]
         acts = []
@@ -99,7 +88,10 @@
             y0 = buf[pl.ds(base, PIECE, stride=2), :] + d0
             y1 = buf[pl.ds(base + 1, PIECE, stride=2), :] + d1
             acts.append(jnp.concatenate([act_of(y0), act_of(y1)], axis=1).astype(BF16))
-        w = scale_of(mm(jnp.concatenate(acts, axis=0), mc[...]))
+        y = mm(jnp.concatenate(acts, axis=0), mc[...])
+        lo = y[:, :L]
+        hi = y[:, L:]
+        w = lax.rsqrt(jnp.sum(lo * lo + hi * hi, axis=1, keepdims=True) + EPS)
         acc0 = acc1 = None
         for k in range(K):
             wk = w[k * PIECE : (k + 1) * PIECE]
@@ -111,6 +103,7 @@
         z[pl.ds(zrow + i0, PIECE), :] = jnp.concatenate([acc0, acc1], axis=1).astype(BF16)
 
     z[...] = jnp.zeros(z.shape, BF16)
+    dst[pl.ds(0, PAIR), :] = receivers(0)
     for s in range(UNROLL):
         fetch(s, s).start()
     fetch(0, 0).wait()
@@ -122,18 +115,18 @@
         for g in range(UNROLL):
             c = t * UNROLL + g
             nxt = (g + 1) % UNROLL
-            node = pl.multiple_of(c * C, C)
             if g % HALF == 0:
                 for s in range(HALF):
                     fetch(c + 1 + s, (nxt + s) % UNROLL).wait()
                 part = g // HALF
                 pair = t * (UNROLL // HALF) + part
+                dst[pl.ds((1 - part) * PAIR, PAIR), :] = receivers(jnp.minimum(pair + 1, nc // HALF - 1))
                 post(pair - 1, 1 - part)
                 finish(pair - 2, part)
             for p in range(C // PIECE):
                 for k in range(p * PIECE * K // C, (p + 1) * PIECE * K // C):
                     gather(slots[nxt], bufs[(g + 1) % 2], k)
-                piece(bufs[g % 2], node, p * PIECE, g * C)
+                piece(bufs[g % 2], p * PIECE, g * C)
             if g % HALF == HALF - 1:
                 for s in range(HALF):
                     n = c + 1 + UNROLL - HALF + 1 + s
@@ -149,19 +142,18 @@
         fetch(0, s).wait()
 
 
-PAIR = HALF * C
-
-
 def level1_kernel(
     base_ref, nbr, mask, owner, h1, prev, nxt, a1, b1, m1, u1, a_up, m_up, h1a, part, send_lo, send_hi,
-    ext, tab, dst, idx_vm, s0, s1, s2, s3, r0, r1, z, msg, mc, mu, ma, mupc, fsem, csem
+    ext, tab, dst, idx_vm, s0, s1, s2, s3, r0, r1, z, msg, mc, mu, ma, mupc, bh, fsem, csem
 ):
     nodes = h1a.shape[0]
     rows = ext.shape[0]
-    loads = [(h1, REACH1, nodes), (prev, 0, REACH1), (nxt, REACH1 + nodes, REACH1)]
+    cut = nodes // 4
+    loads = [(h1, q * cut, REACH1 + q * cut, cut) for q in range(4)]
+    loads += [(prev, 0, 0, REACH1), (nxt, 0, REACH1 + nodes, REACH1)]
     copies = [
-        pltpu.make_async_copy(src, ext.at[pl.ds(at, n), :], csem.at[i])
-        for i, (src, at, n) in enumerate(loads)
+        pltpu.make_async_copy(src.at[pl.ds(off, n), :], ext.at[pl.ds(at, n), :], csem.at[i])
+        for i, (src, off, at, n) in enumerate(loads)
     ]
     for cp in copies:
         cp.start()
@@ -172,16 +164,21 @@
         row = nbr[:, cols] + (lane + (REACH1 + c * C))
         idx_vm[c] = 2 * jnp.where(mask[:, cols] > 0, row, rows)
     mcv = centered(m1)
-    mc[...] = mcv
+    mc[...] = mcv * (1.0 / 16.0)
     mu[...] = mm(mcv, u1[...]).astype(BF16)
     ma[...] = half(a_up)
     mupc[...] = centered(m_up)
     part[...] = jnp.zeros(part.shape, F32)
     msg[...] = jnp.zeros(msg.shape, BF16)
-    for cp in copies:
+    ah = half(a1)
+    bh[...] = half(b1)
+    for cp, (_, _, at, n) in zip(copies, loads):
         cp.wait()
-    build_table(tab, ext, half(a1), rows)
-    build_dst(dst, ext, REACH1, half(b1), nodes)
+        build_table(tab, ext, ah, at, n)
+    tab[pl.ds(2 * rows, 8), :] = jnp.full((8, L), DEAD, F32)
+
+    def receivers(pair):
+        return mm(ext[pl.ds(pl.multiple_of(pair * PAIR, PAIR) + REACH1, PAIR), :], bh[...])
 
     def post(step, at):
         node = pl.multiple_of(jnp.maximum(step, 0) * PAIR, PAIR)
@@ -211,7 +208,7 @@
         )
 
     edge_loop(
-        nodes // C, idx_vm, (s0, s1, s2, s3), fsem, (r0, r1), tab, dst, mc, z, post, finish
+        nodes // C, idx_vm, (s0, s1, s2, s3), fsem, (r0, r1), tab, dst, mc, z, receivers, post, finish
     )
     n = 2 * REACH2
     send_lo[...] = part[pl.ds(0, n), :].astype(BF16)
@@ -229,7 +226,7 @@
 def gather_scratch(rows, nodes):
     return [
         pltpu.VMEM((2 * rows + 8, L), F32),
-        pltpu.VMEM((nodes, W), F32),
+        pltpu.VMEM((2 * PAIR, W), F32),
         pltpu.VMEM((nodes // C, K, L), jnp.int32),
         *[pltpu.SMEM((K, L), jnp.int32) for _ in range(UNROLL)],
         *[pltpu.VMEM((2 * K * C, L), F32) for _ in range(2)],
@@ -260,9 +257,9 @@
             pltpu.VMEM((rows, W), BF16),
             *gather_scratch(rows, nodes),
             pltpu.VMEM((UNROLL * C, W), BF16),
-            *[pltpu.VMEM((W, W), BF16) for _ in range(4)],
+            *[pltpu.VMEM((W, W), BF16) for _ in range(5)],
             pltpu.SemaphoreType.DMA((UNROLL,)),
-            pltpu.SemaphoreType.DMA((3,)),
+            pltpu.SemaphoreType.DMA((6,)),
         ],
         compiler_params=pltpu.CompilerParams(vmem_limit_bytes=VMEM_BYTES),
         cost_estimate=pl.CostEstimate(
@@ -274,7 +271,7 @@
 
 def level2_kernel(
     base_ref, nbr, mask, part, from_lo, from_hi, h2, lo2, hi2, u2, a2, b2, m2, v2, h2o, edge_lo, edge_hi,
-    h2x, tab, dst, idx_vm, s0, s1, s2, s3, r0, r1, z, mc, mv, fsem
+    h2x, tab, dst, idx_vm, s0, s1, s2, s3, r0, r1, z, mc, mv, bh, fsem
 ):
     n2 = h2o.shape[0]
     rows = n2 + 2 * REACH2
@@ -304,10 +301,14 @@
         row = nbr[:, cols] - (base - REACH2)
         idx_vm[c] = 2 * jnp.where(mask[:, cols] > 0, row, rows)
     mcv = centered(m2)
-    mc[...] = mcv
+    mc[...] = mcv * (1.0 / 16.0)
     mv[...] = mm(mcv, v2[...]).astype(BF16)
-    build_table(tab, h2x, half(a2), rows)
-    build_dst(dst, h2x, REACH2, half(b2), n2)
+    build_table(tab, h2x, half(a2), 0, rows)
+    tab[pl.ds(2 * rows, 8), :] = jnp.full((8, L), DEAD, F32)
+    bh[...] = half(b2)
+
+    def receivers(pair):
+        return mm(h2x[pl.ds(pl.multiple_of(pair * PAIR, PAIR) + REACH2, PAIR), :], bh[...])
 
     def post(step, at):
         node = pl.multiple_of(jnp.maximum(step, 0) * PAIR, PAIR)
@@ -315,7 +316,7 @@
         h2o[pl.ds(node, PAIR), :] = (hrow + mm(z[pl.ds(at * PAIR, PAIR), :], mv[...])).astype(BF16)
 
     edge_loop(
-        n2 // C, idx_vm, (s0, s1, s2, s3), fsem, (r0, r1), tab, dst, mc, z, post, lambda p, at: None
+        n2 // C, idx_vm, (s0, s1, s2, s3), fsem, (r0, r1), tab, dst, mc, z, receivers, post, lambda p, at: None
     )
     edge_lo[...] = h2o[pl.ds(0, REACH2), :]
     edge_hi[...] = h2o[pl.ds(n2 - REACH2, REACH2), :]
@@ -329,13 +330,16 @@
     return pl.pallas_call(
         level2_kernel,
         out_shape=[shape((nodes, W), BF16), shape((REACH2, W), BF16), shape((REACH2, W), BF16)],
-        in_specs=[pl.BlockSpec(memory_space=pltpu.SMEM)] + [vmem()] * (len(args) - 1),
+        grid=(1,),
+        in_specs=[pl.BlockSpec(memory_space=pltpu.SMEM)]
+        + [vmem()] * 6
+        + [pl.BlockSpec((REACH2, W), lambda t: (REACH1 // REACH2, 0))] * 2
+        + [vmem()] * len(weights),
         out_specs=[vmem()] * 3,
         scratch_shapes=[
             pltpu.VMEM((rows, W), BF16),
             *gather_scratch(rows, nodes),
-            pltpu.VMEM((W, W), BF16),
-            pltpu.VMEM((W, W), BF16),
+            *[pltpu.VMEM((W, W), BF16) for _ in range(3)],
             pltpu.SemaphoreType.DMA((UNROLL,)),
         ],
         compiler_params=pltpu.CompilerParams(vmem_limit_bytes=VMEM_BYTES),
@@ -462,14 +466,17 @@
     base = jnp.reshape(device * nodes2, (1,)).astype(jnp.int32)
     nbr1_t, mask1_t, nbr2_t, mask2_t = nbr1.T, mask1.T, nbr2.T, mask2.T
     owner2 = owner.reshape(nodes1 // L, L)
-    halo1 = swap(h1[nodes1 - REACH1 :], h1[:REACH1], ("grp", "sub"))
-    halo2 = swap(h2[nodes2 - REACH2 :], h2[:REACH2], "sub")
+    halo = swap(
+        jnp.concatenate([h1[nodes1 - REACH1 :], h2[nodes2 - REACH2 :]], axis=0),
+        jnp.concatenate([h1[:REACH1], h2[:REACH2]], axis=0),
+        ("grp", "sub"),
+    )
     h1a, part, send_lo, send_hi = level1(
-        base, nbr1_t, mask1_t, owner2, h1, *halo1, (a1, b1, m1, u1, a_up, m_up)
+        base, nbr1_t, mask1_t, owner2, h1, *halo, (a1, b1, m1, u1, a_up, m_up)
     )
     from_lo, from_hi = swap(send_hi, send_lo, "sub")
     h2_out, edge_lo, edge_hi = level2(
-        base, nbr2_t, mask2_t, part, from_lo, from_hi, h2, *halo2, (u2, a2, b2, m2, v2)
+        base, nbr2_t, mask2_t, part, from_lo, from_hi, h2, *halo, (u2, a2, b2, m2, v2)
     )
     lo, hi = swap(edge_hi, edge_lo, "sub")
     h1_out = down(base, owner2, h1a, h2_out, lo, hi, a_down, b_down, m_down)

time: 182 us -> 167 us (0.918)
  starting transfers between devices: 38.4 us -> 14.8 us
  waiting for transfers between devices: 16 us -> 30.2 us
  Pallas kernels: 122 us -> 117 us
    ppermute x4 -> x3, starting transfers between devices: 29.9 us -> 7.86 us  [swap(): lax.ppermute(to_next, axis, [(i, (i + 1) % count) for i in range(ends)])]
    ppermute x4 -> x3, waiting for transfers between devices: 13.6 us -> 23.6 us  [swap(): lax.ppermute(to_prev, axis, [((i + 1) % count, i) for i in range(ends)])]
    pallas_call x1, Pallas kernels: 84.3 us -> 80.1 us  [level1(): pl.pallas_call(level1_kernel, out_shape=[shape((nodes, W), BF16), shape((...]
    ppermute x4 -> x3, waiting for transfers between devices: 2.43 us -> 6.54 us  [swap(): lax.ppermute(to_next, axis, [(i, (i + 1) % count) for i in range(ends)])]
    ppermute x4 -> x3, starting transfers between devices: 8.52 us -> 6.91 us  [swap(): lax.ppermute(to_prev, axis, [((i + 1) % count, i) for i in range(ends)])]
  transfers between devices with their start and end apart: 8 -> 6, of which waited for: 6 -> 5; matrix products, arithmetic and copies ran while one was open for 1% -> 0% of each run, Pallas kernels for 0% -> 0%
where the time goes in v1:
time: 167 us
  Pallas kernels  117 us (70%)
  waiting for transfers between devices  30.2 us (18%)
  starting transfers between devices  14.8 us (9%)
  local copies, waits for them, and re-layouts  4.48 us (3%)
    pallas_call x1, Pallas kernels, level1(): pl.pallas_call(level1_kernel, out_shape=[shape((nodes, W), BF16), shape((...  80.1 us
    ppermute x3, waiting for transfers between devices, swap(): lax.ppermute(to_prev, axis, [((i + 1) % count, i) for i in range(ends)])  23.6 us
    pallas_call x1, Pallas kernels, level2(): pl.pallas_call(level2_kernel, out_shape=[shape((nodes, W), BF16), shape((...  21.8 us
    pallas_call x1, Pallas kernels, down(): pl.pallas_call(down_kernel, grid=(nodes1 // DOWN,), out_shape=jax.ShapeDt...  14.9 us
    ppermute x3, starting transfers between devices, swap(): lax.ppermute(to_next, axis, [(i, (i + 1) % count) for i in range(ends)])  7.86 us
    ppermute x3, starting transfers between devices, swap(): lax.ppermute(to_prev, axis, [((i + 1) % count, i) for i in range(ends)])  6.91 us
    ppermute x3, waiting for transfers between devices, swap(): lax.ppermute(to_next, axis, [(i, (i + 1) % count) for i in range(ends)])  6.54 us
  transfers between devices with their start and end apart: 6, of which 5 were waited for; matrix products, arithmetic and copies ran while one was open for 0% of the time, Pallas kernels for 0%

profile of v1, /device:TPU:103, one launch (start us, length us, event | category | flops | bytes accessed | tf_op | source)
XLA Modules:
  0.0 167.0 jit_solution(12682090329408170109)
XLA Ops:
  0.6 1.0 fusion.1
  1.6 1.3 fusion
  2.9 4.0 %collective-permute-start = (bf16[1280,256]{1,0:T(8,128)(2,1)S(1)}, bf16[1280,256]{1,0:T(8,128)(2,1)S(1)}, u32[]{:S(2)}, u32[]{:S(2)}) collective-permute-start(bf16[1280,256]{1,0:T(8,128)(2,1)S(1)} %pad_maximum_fusion), channel_id=1, source_target_pairs={{0,1},{1,2},{2,3},{3,4},{4,5},{5,6},{6,7},{7,8},{8,9},{9,10},{10,1... | collective-permute-start | bytes 1966088 | tf_op jit(solution)/shard_map/ppermute | solution.py:435
  7.0 1.9 %collective-permute-start.1 = (bf16[1280,256]{1,0:T(8,128)(2,1)S(1)}, bf16[1280,256]{1,0:T(8,128)(2,1)S(1)}, u32[]{:S(2)}, u32[]{:S(2)}) collective-permute-start(bf16[1280,256]{1,0:T(8,128)(2,1)S(1)} %pad_maximum_fusion.1), channel_id=1, source_target_pairs={{1,0},{2,1},{3,2},{4,3},{5,4},{6,5},{7,6},{8,7},{9,8},{10,9},{11,1... | collective-permute-start | bytes 1966088 | tf_op jit(solution)/shard_map/ppermute | solution.py:436
  9.0 5.5 %collective-permute-done.prev.lo2 = bf16[1280,256]{1,0:T(8,128)(2,1)S(1)} collective-permute-done((bf16[1280,256]{1,0:T(8,128)(2,1)S(1)}, bf16[1280,256]{1,0:T(8,128)(2,1)S(1)}, u32[]{:S(2)}, u32[]{:S(2)}) %collective-permute-start) | collective-permute-done | bytes 655392 | tf_op jit(solution)/shard_map/ppermute | solution.py:435
  14.5 0.0 copy-start
  14.5 8.1 %collective-permute-done.1.nxt.hi2 = bf16[1280,256]{1,0:T(8,128)(2,1)S(1)} collective-permute-done((bf16[1280,256]{1,0:T(8,128)(2,1)S(1)}, bf16[1280,256]{1,0:T(8,128)(2,1)S(1)}, u32[]{:S(2)}, u32[]{:S(2)}) %collective-permute-start.1) | collective-permute-done | bytes 655392 | tf_op jit(solution)/shard_map/ppermute | solution.py:436
  22.5 0.0 copy-start.1
  22.5 0.0 copy-done
  22.5 0.9 copy-done.1
  23.4 80.1 %level1.1 = (bf16[8192,256]{1,0:T(8,128)(2,1)}, f32[2560,256]{1,0:T(8,128)}, bf16[512,256]{1,0:T(8,128)(2,1)}, bf16[512,256]{1,0:T(8,128)(2,1)}) custom-call(s32[1]{0:T(128)} %bitcast.base_ref, s32[8,8192]{1,0:T(8,128)} %bitcast.6, s32[8,8192]{1,0:T(8,128)} %bitcast.7, s32[64,128]{1,0:T(8,128)} %bitcast.10, bf16[8192,256]{1,0:T(8,128)(2,1)} %h1.1, ...), custom_call_target="tpu_custom_call" | custom-call | flops 17179869184 | bytes 10485760 | tf_op jit(solution)/shard_map/level1/pallas_call | solution.py:243
  103.5 1.9 %collective-permute-start.2 = (bf16[512,256]{1,0:T(8,128)(2,1)}, bf16[512,256]{1,0:T(8,128)(2,1)S(1)}, u32[]{:S(2)}, u32[]{:S(2)}) collective-permute-start(bf16[512,256]{1,0:T(8,128)(2,1)} %get-tuple-element.11), channel_id=1, source_target_pairs={{0,1},{1,2},{2,3},{3,4},{4,5},{5,6},{6,7},{7,8},{8,9},{9,10},{10,1... | collective-permute-start | bytes 786440 | tf_op jit(solution)/shard_map/ppermute | solution.py:435
  105.4 2.6 %collective-permute-start.3 = (bf16[512,256]{1,0:T(8,128)(2,1)}, bf16[512,256]{1,0:T(8,128)(2,1)S(1)}, u32[]{:S(2)}, u32[]{:S(2)}) collective-permute-start(bf16[512,256]{1,0:T(8,128)(2,1)} %get-tuple-element.12), channel_id=1, source_target_pairs={{1,0},{2,1},{3,2},{4,3},{5,4},{6,5},{7,6},{8,7},{9,8},{10,9},{11,1... | collective-permute-start | bytes 786440 | tf_op jit(solution)/shard_map/ppermute | solution.py:436
  108.0 1.0 collective-permute-done.2.from_lo
  109.0 0.0 copy-start.2
  109.0 7.9 %collective-permute-done.3.from_hi = bf16[512,256]{1,0:T(8,128)(2,1)S(1)} collective-permute-done((bf16[512,256]{1,0:T(8,128)(2,1)}, bf16[512,256]{1,0:T(8,128)(2,1)S(1)}, u32[]{:S(2)}, u32[]{:S(2)}) %collective-permute-start.3) | collective-permute-done | bytes 262176 | tf_op jit(solution)/shard_map/ppermute | solution.py:436
  116.9 0.0 copy-start.3
  116.9 0.0 copy-done.2
  116.9 0.7 copy-done.3
  117.6 21.8 %level2.1 = (bf16[2048,256]{1,0:T(8,128)(2,1)}, bf16[256,256]{1,0:T(8,128)(2,1)}, bf16[256,256]{1,0:T(8,128)(2,1)}) custom-call(s32[1]{0:T(128)} %bitcast.base_ref, s32[8,2048]{1,0:T(8,128)} %bitcast.8, s32[8,2048]{1,0:T(8,128)} %bitcast.9, f32[2560,256]{1,0:T(8,128)} %get-tuple-element.10.part, bf16[512,256]{1,0:T(8,128)(2,1)} %copy-done.2, ...), custom_call_target="tpu_custom_call" | custom-call | flops 4294967296 | bytes 2621440 | tf_op jit(solution)/shard_map/level2/pallas_call | solution.py:330
  139.4 1.9 %collective-permute-start.4 = (bf16[256,256]{1,0:T(8,128)(2,1)}, bf16[256,256]{1,0:T(8,128)(2,1)S(1)}, u32[]{:S(2)}, u32[]{:S(2)}) collective-permute-start(bf16[256,256]{1,0:T(8,128)(2,1)} %get-tuple-element.14), channel_id=1, source_target_pairs={{0,1},{1,2},{2,3},{3,4},{4,5},{5,6},{6,7},{7,8},{8,9},{9,10},{10,1... | collective-permute-start | bytes 393224 | tf_op jit(solution)/shard_map/ppermute | solution.py:435
  141.3 2.4 %collective-permute-start.5 = (bf16[256,256]{1,0:T(8,128)(2,1)}, bf16[256,256]{1,0:T(8,128)(2,1)S(1)}, u32[]{:S(2)}, u32[]{:S(2)}) collective-permute-start(bf16[256,256]{1,0:T(8,128)(2,1)} %get-tuple-element.15), channel_id=1, source_target_pairs={{1,0},{2,1},{3,2},{4,3},{5,4},{6,5},{7,6},{8,7},{9,8},{10,9},{11,1... | collective-permute-start | bytes 393224 | tf_op jit(solution)/shard_map/ppermute | solution.py:436
  143.7 0.0 collective-permute-done.4.lo
  143.7 0.0 copy-start.4
  143.8 7.7 %collective-permute-done.5.hi = bf16[256,256]{1,0:T(8,128)(2,1)S(1)} collective-permute-done((bf16[256,256]{1,0:T(8,128)(2,1)}, bf16[256,256]{1,0:T(8,128)(2,1)S(1)}, u32[]{:S(2)}, u32[]{:S(2)}) %collective-permute-start.5) | collective-permute-done | bytes 131104 | tf_op jit(solution)/shard_map/ppermute | solution.py:436
  151.4 0.0 copy-start.5
  151.4 0.0 copy-done.4
  151.4 0.7 copy-done.5
  152.1 14.9 %down.1 = bf16[8192,256]{1,0:T(8,128)(2,1)} custom-call(s32[1]{0:T(128)} %bitcast.base_ref, s32[64,128]{1,0:T(8,128)} %bitcast.11, bf16[8192,256]{1,0:T(8,128)(2,1)} %get-tuple-element.9.h1a, bf16[2048,256]{1,0:T(8,128)(2,1)} %get-tuple-element.8.h2o, bf16[256,256]{1,0:T(8,128)(2,1)} %copy-done.4, bf16[256,256]{1,0:T(8,128)(2,1)} %copy-done.5, ...), custom_call_target="tpu_custom_call" | custom-call | flops 5368709120 | bytes 8388608 | tf_op jit(solution)/shard_map/down/pallas_call | solution.py:403
  (2 shorter events, 0.1 us)
Async XLA Ops:
  2.9 11.5 %collective-permute-start = (bf16[1280,256]{1,0:T(8,128)(2,1)S(1)}, bf16[1280,256]{1,0:T(8,128)(2,1)S(1)}, u32[]{:S(2)}, u32[]{:S(2)}) collective-permute-start(bf16[1280,256]{1,0:T(8,128)(2,1)S(1)} %pad_maximum_fusion), channel_id=1, source_target_pairs={{0,1},{1,2},{2,3},{3,4},{4,5},{5,6},{6,7},{7,8},{8,9},{9,10},{10,1... | collective-permute-start | bytes 1966088 | tf_op jit(solution)/shard_map/ppermute | solution.py:435
  7.0 15.5 %collective-permute-start.1 = (bf16[1280,256]{1,0:T(8,128)(2,1)S(1)}, bf16[1280,256]{1,0:T(8,128)(2,1)S(1)}, u32[]{:S(2)}, u32[]{:S(2)}) collective-permute-start(bf16[1280,256]{1,0:T(8,128)(2,1)S(1)} %pad_maximum_fusion.1), channel_id=1, source_target_pairs={{1,0},{2,1},{3,2},{4,3},{5,4},{6,5},{7,6},{8,7},{9,8},{10,9},{11,1... | collective-permute-start | bytes 1966088 | tf_op jit(solution)/shard_map/ppermute | solution.py:436
  14.5 8.1 %copy-start = (bf16[1280,256]{1,0:T(8,128)(2,1)}, bf16[1280,256]{1,0:T(8,128)(2,1)S(1)}, u32[]{:S(2)}) copy-start(bf16[1280,256]{1,0:T(8,128)(2,1)S(1)} %collective-permute-done.prev.lo2) | copy-start | bytes 1966084
  22.5 0.9 copy-start.1
  103.5 5.5 %collective-permute-start.2 = (bf16[512,256]{1,0:T(8,128)(2,1)}, bf16[512,256]{1,0:T(8,128)(2,1)S(1)}, u32[]{:S(2)}, u32[]{:S(2)}) collective-permute-start(bf16[512,256]{1,0:T(8,128)(2,1)} %get-tuple-element.11), channel_id=1, source_target_pairs={{0,1},{1,2},{2,3},{3,4},{4,5},{5,6},{6,7},{7,8},{8,9},{9,10},{10,1... | collective-permute-start | bytes 786440 | tf_op jit(solution)/shard_map/ppermute | solution.py:435
  105.4 11.5 %collective-permute-start.3 = (bf16[512,256]{1,0:T(8,128)(2,1)}, bf16[512,256]{1,0:T(8,128)(2,1)S(1)}, u32[]{:S(2)}, u32[]{:S(2)}) collective-permute-start(bf16[512,256]{1,0:T(8,128)(2,1)} %get-tuple-element.12), channel_id=1, source_target_pairs={{1,0},{2,1},{3,2},{4,3},{5,4},{6,5},{7,6},{8,7},{9,8},{10,9},{11,1... | collective-permute-start | bytes 786440 | tf_op jit(solution)/shard_map/ppermute | solution.py:436
  109.0 7.9 %copy-start.2 = (bf16[512,256]{1,0:T(8,128)(2,1)}, bf16[512,256]{1,0:T(8,128)(2,1)S(1)}, u32[]{:S(2)}) copy-start(bf16[512,256]{1,0:T(8,128)(2,1)S(1)} %collective-permute-done.2.from_lo) | copy-start | bytes 786436
  116.9 0.7 copy-start.3
  139.4 4.3 %collective-permute-start.4 = (bf16[256,256]{1,0:T(8,128)(2,1)}, bf16[256,256]{1,0:T(8,128)(2,1)S(1)}, u32[]{:S(2)}, u32[]{:S(2)}) collective-permute-start(bf16[256,256]{1,0:T(8,128)(2,1)} %get-tuple-element.14), channel_id=1, source_target_pairs={{0,1},{1,2},{2,3},{3,4},{4,5},{5,6},{6,7},{7,8},{8,9},{9,10},{10,1... | collective-permute-start | bytes 393224 | tf_op jit(solution)/shard_map/ppermute | solution.py:435
  141.3 10.1 %collective-permute-start.5 = (bf16[256,256]{1,0:T(8,128)(2,1)}, bf16[256,256]{1,0:T(8,128)(2,1)S(1)}, u32[]{:S(2)}, u32[]{:S(2)}) collective-permute-start(bf16[256,256]{1,0:T(8,128)(2,1)} %get-tuple-element.15), channel_id=1, source_target_pairs={{1,0},{2,1},{3,2},{4,3},{5,4},{6,5},{7,6},{8,7},{9,8},{10,9},{11,1... | collective-permute-start | bytes 393224 | tf_op jit(solution)/shard_map/ppermute | solution.py:436
  143.7 7.7 %copy-start.4 = (bf16[256,256]{1,0:T(8,128)(2,1)}, bf16[256,256]{1,0:T(8,128)(2,1)S(1)}, u32[]{:S(2)}) copy-start(bf16[256,256]{1,0:T(8,128)(2,1)S(1)} %collective-permute-done.4.lo) | copy-start | bytes 393220
  151.4 0.7 copy-start.5

commit v2 on v1

--- a/solution.py
+++ b/solution.py
@@ -39,6 +39,14 @@
 
 def act_of(y):
     return y + y * jnp.tanh(y)
+
+
+def is_odd(base_ref, n2):
+    return lax.rem(lax.div(base_ref[0], n2), 2) == 1
+
+
+def pick(odd, a, b):
+    return jnp.where(odd, a.astype(F32), b.astype(F32))
 
 
 def ones_block():
@@ -143,14 +151,17 @@
 
 
 def level1_kernel(
-    base_ref, nbr, mask, owner, h1, prev, nxt, a1, b1, m1, u1, a_up, m_up, h1a, part, send_lo, send_hi,
+    base_ref, nbr, mask, owner, h1, near, far, a1, b1, m1, u1, a_up, m_up, h1a, part, inner, outer,
     ext, tab, dst, idx_vm, s0, s1, s2, s3, r0, r1, z, msg, mc, mu, ma, mupc, bh, fsem, csem
 ):
     nodes = h1a.shape[0]
     rows = ext.shape[0]
     cut = nodes // 4
     loads = [(h1, q * cut, REACH1 + q * cut, cut) for q in range(4)]
-    loads += [(prev, 0, 0, REACH1), (nxt, 0, REACH1 + nodes, REACH1)]
+    odd = is_odd(base_ref, nodes // 4)
+    near_at = pl.multiple_of(jnp.where(odd, 0, REACH1 + nodes), REACH1)
+    far_at = pl.multiple_of(jnp.where(odd, REACH1 + nodes, 0), REACH1)
+    loads += [(near, 0, near_at, REACH1), (far, 0, far_at, REACH1)]
     copies = [
         pltpu.make_async_copy(src.at[pl.ds(off, n), :], ext.at[pl.ds(at, n), :], csem.at[i])
         for i, (src, off, at, n) in enumerate(loads)
@@ -211,8 +222,10 @@
         nodes // C, idx_vm, (s0, s1, s2, s3), fsem, (r0, r1), tab, dst, mc, z, receivers, post, finish
     )
     n = 2 * REACH2
-    send_lo[...] = part[pl.ds(0, n), :].astype(BF16)
-    send_hi[...] = part[pl.ds(part.shape[0] - n, n), :].astype(BF16)
+    low = part[pl.ds(0, n), :]
+    up = part[pl.ds(part.shape[0] - n, n), :]
+    inner[...] = pick(odd, low, up).astype(BF16)
+    outer[...] = pick(odd, up, low).astype(BF16)
 
 
 def vmem():
@@ -270,26 +283,27 @@
 
 
 def level2_kernel(
-    base_ref, nbr, mask, part, from_lo, from_hi, h2, lo2, hi2, u2, a2, b2, m2, v2, h2o, edge_lo, edge_hi,
+    base_ref, nbr, mask, part, inner, outer, h2, near2, far2, u2, a2, b2, m2, v2, h2o, edge_in, edge_out,
     h2x, tab, dst, idx_vm, s0, s1, s2, s3, r0, r1, z, mc, mv, bh, fsem
 ):
     n2 = h2o.shape[0]
     rows = n2 + 2 * REACH2
     S = 2 * REACH2
+    odd = is_odd(base_ref, n2)
     u = u2[...]
     for q in range(rows // S):
         piece = part[pl.ds(q * S, S), :]
         if q == 0:
-            piece = piece + from_lo[...].astype(F32)
+            piece = piece + pick(odd, inner[...], outer[...])
         elif q == rows // S - 1:
-            piece = piece + from_hi[...].astype(F32)
+            piece = piece + pick(odd, outer[...], inner[...])
         d = mm(piece.astype(BF16), u)
         for hf in range(2):
             at = q * S + hf * REACH2
             if at == 0:
-                src = lo2[...]
+                src = pick(odd, near2[...], far2[...])
             elif at == rows - REACH2:
-                src = hi2[...]
+                src = pick(odd, far2[...], near2[...])
             else:
                 src = h2[pl.ds(at - REACH2, REACH2), :]
             dd = d[hf * REACH2 : (hf + 1) * REACH2]
@@ -318,8 +332,10 @@
     edge_loop(
         n2 // C, idx_vm, (s0, s1, s2, s3), fsem, (r0, r1), tab, dst, mc, z, receivers, post, lambda p, at: None
     )
-    edge_lo[...] = h2o[pl.ds(0, REACH2), :]
-    edge_hi[...] = h2o[pl.ds(n2 - REACH2, REACH2), :]
+    low = h2o[pl.ds(0, REACH2), :]
+    up = h2o[pl.ds(n2 - REACH2, REACH2), :]
+    edge_in[...] = pick(odd, low, up).astype(BF16)
+    edge_out[...] = pick(odd, up, low).astype(BF16)
 
 
 def level2(base, nbr_t, mask_t, part, from_lo, from_hi, h2, lo2, hi2, weights):
@@ -354,17 +370,20 @@
 GROUP = 512
 
 
-def down_kernel(base_ref, owner, h1a, h2o, lo, hi, a_down, b_down, m_down, o_ref, pd, bd, mdc):
+def down_kernel(base_ref, owner, h1a, h2o, near, far, a_down, b_down, m_down, o_ref, pd, bd, mdc):
     t = pl.program_id(0)
     n2 = h2o.shape[0]
 
     @pl.when(t == 0)
     def _():
         a = half(a_down)
-        pd[pl.ds(0, REACH2), :] = mm(lo[...], a).astype(BF16)
+        odd = is_odd(base_ref, n2)
+        low = pick(odd, near[...], far[...]).astype(BF16)
+        up = pick(odd, far[...], near[...]).astype(BF16)
+        pd[pl.ds(0, REACH2), :] = mm(low, a).astype(BF16)
         for b in range(n2 // 256):
             pd[pl.ds(REACH2 + b * 256, 256), :] = mm(h2o[pl.ds(b * 256, 256), :], a).astype(BF16)
-        pd[pl.ds(REACH2 + n2, REACH2), :] = mm(hi[...], a).astype(BF16)
+        pd[pl.ds(REACH2 + n2, REACH2), :] = mm(up, a).astype(BF16)
         bd[...] = half(b_down)
         mdc[...] = centered(m_down)
 
@@ -429,12 +448,14 @@
     )(base, owner2, h1a, h2o, lo, hi, a_down, b_down, m_down)
 
 
-def swap(to_next, to_prev, axis):
+def swap(inner, outer, axis):
     count = lax.axis_size(axis)
-    ends = count - 1
-    from_prev = lax.ppermute(to_next, axis, [(i, (i + 1) % count) for i in range(ends)])
-    from_next = lax.ppermute(to_prev, axis, [((i + 1) % count, i) for i in range(ends)])
-    return from_prev, from_next
+
+    def both(first):
+        pairs = [(i, i + 1) for i in range(first, count - 1, 2)]
+        return pairs + [(j, i) for i, j in pairs]
+
+    return lax.ppermute(inner, axis, both(0)), lax.ppermute(outer, axis, both(1))
 
 
 def shards(
@@ -466,20 +487,19 @@
     base = jnp.reshape(device * nodes2, (1,)).astype(jnp.int32)
     nbr1_t, mask1_t, nbr2_t, mask2_t = nbr1.T, mask1.T, nbr2.T, mask2.T
     owner2 = owner.reshape(nodes1 // L, L)
-    halo = swap(
-        jnp.concatenate([h1[nodes1 - REACH1 :], h2[nodes2 - REACH2 :]], axis=0),
-        jnp.concatenate([h1[:REACH1], h2[:REACH2]], axis=0),
-        ("grp", "sub"),
-    )
-    h1a, part, send_lo, send_hi = level1(
+    up = jnp.concatenate([h1[nodes1 - REACH1 :], h2[nodes2 - REACH2 :]], axis=0)
+    low = jnp.concatenate([h1[:REACH1], h2[:REACH2]], axis=0)
+    odd = device % 2 == 1
+    halo = swap(jnp.where(odd, low, up), jnp.where(odd, up, low), ("grp", "sub"))
+    h1a, part, inner, outer = level1(
         base, nbr1_t, mask1_t, owner2, h1, *halo, (a1, b1, m1, u1, a_up, m_up)
     )
-    from_lo, from_hi = swap(send_hi, send_lo, "sub")
-    h2_out, edge_lo, edge_hi = level2(
-        base, nbr2_t, mask2_t, part, from_lo, from_hi, h2, *halo, (u2, a2, b2, m2, v2)
+    inner, outer = swap(inner, outer, "sub")
+    h2_out, edge_in, edge_out = level2(
+        base, nbr2_t, mask2_t, part, inner, outer, h2, *halo, (u2, a2, b2, m2, v2)
     )
-    lo, hi = swap(edge_hi, edge_lo, "sub")
-    h1_out = down(base, owner2, h1a, h2_out, lo, hi, a_down, b_down, m_down)
+    edge_in, edge_out = swap(edge_in, edge_out, "sub")
+    h1_out = down(base, owner2, h1a, h2_out, edge_in, edge_out, a_down, b_down, m_down)
     return (h1_out, h2_out)
 
 

time: 167 us -> 160 us (0.958)
  waiting for transfers between devices: 30.2 us -> 24.8 us
  starting transfers between devices: 14.8 us -> 12.5 us
    ppermute x6, waiting for transfers between devices: 30.2 us -> 24.8 us  [the longest x3 24.8 us: swap(): lax.ppermute(outer, axis, both(1))]
    ppermute x6, starting transfers between devices: 14.8 us -> 12.5 us  [the longest x3 12.2 us: swap(): lax.ppermute(outer, axis, both(1))]
  transfers between devices with their start and end apart: 6 -> 6, of which waited for: 5 -> 3; matrix products, arithmetic and copies ran while one was open for 0% -> 0% of each run, Pallas kernels for 0% -> 0%
where the time goes in v2:
time: 160 us
  Pallas kernels  117 us (73%)
  waiting for transfers between devices  24.8 us (16%)
  starting transfers between devices  12.5 us (8%)
  local copies, waits for them, and re-layouts  4.69 us (3%)
    pallas_call x1, Pallas kernels, level1(): pl.pallas_call(level1_kernel, out_shape=[shape((nodes, W), BF16), shape((...  80.4 us
    ppermute x3, waiting for transfers between devices, swap(): lax.ppermute(outer, axis, both(1))  24.8 us
    pallas_call x1, Pallas kernels, level2(): pl.pallas_call(level2_kernel, out_shape=[shape((nodes, W), BF16), shape((...  21.8 us
    pallas_call x1, Pallas kernels, down(): pl.pallas_call(down_kernel, grid=(nodes1 // DOWN,), out_shape=jax.ShapeDt...  14.9 us
    ppermute x3, starting transfers between devices, swap(): lax.ppermute(outer, axis, both(1))  12.2 us
  transfers between devices with their start and end apart: 6, of which 3 were waited for; matrix products, arithmetic and copies ran while one was open for 0% of the time, Pallas kernels for 0%

profile of v2, /device:TPU:103, one launch (start us, length us, event | category | flops | bytes accessed | tf_op | source)
XLA Modules:
  0.0 160.0 jit_solution(6647033694023078394)
XLA Ops:
  0.6 1.0 fusion.1
  1.6 1.3 fusion
  2.9 0.3 broadcast_select_fusion
  3.2 4.0 %collective-permute-start.1 = (bf16[1280,256]{1,0:T(8,128)(2,1)S(1)}, bf16[1280,256]{1,0:T(8,128)(2,1)S(1)}, u32[]{:S(2)}, u32[]{:S(2)}) collective-permute-start(bf16[1280,256]{1,0:T(8,128)(2,1)S(1)} %get-tuple-element.18), channel_id=1, source_target_pairs={{1,2},{3,4},{5,6},{7,8},{9,10},{11,12},{13,14},{15,16},{17,18},{19... | collective-permute-start | bytes 1966088 | tf_op jit(solution)/shard_map/ppermute | solution.py:458
  7.2 0.1 collective-permute-start
  7.3 11.4 %collective-permute-done.1.far.far2 = bf16[1280,256]{1,0:T(8,128)(2,1)S(1)} collective-permute-done((bf16[1280,256]{1,0:T(8,128)(2,1)S(1)}, bf16[1280,256]{1,0:T(8,128)(2,1)S(1)}, u32[]{:S(2)}, u32[]{:S(2)}) %collective-permute-start.1) | collective-permute-done | bytes 655392 | tf_op jit(solution)/shard_map/ppermute | solution.py:458
  18.7 0.0 copy-start
  18.7 0.0 collective-permute-done.near.near2
  18.7 0.0 copy-start.1
  18.7 0.8 copy-done
  19.5 0.2 copy-done.1
  19.7 80.4 %level1.1 = (bf16[8192,256]{1,0:T(8,128)(2,1)}, f32[2560,256]{1,0:T(8,128)}, bf16[512,256]{1,0:T(8,128)(2,1)}, bf16[512,256]{1,0:T(8,128)(2,1)}) custom-call(s32[1]{0:T(128)} %bitcast.base_ref, s32[8,8192]{1,0:T(8,128)} %bitcast.6, s32[8,8192]{1,0:T(8,128)} %bitcast.7, s32[64,128]{1,0:T(8,128)} %bitcast.10, bf16[8192,256]{1,0:T(8,128)(2,1)} %h1.1, ...), custom_call_target="tpu_custom_call" | custom-call | flops 17179869184 | bytes 10485760 | tf_op jit(solution)/shard_map/level1/pallas_call | solution.py:256
  100.1 0.1 collective-permute-start.2
  100.2 4.2 %collective-permute-start.3 = (bf16[512,256]{1,0:T(8,128)(2,1)}, bf16[512,256]{1,0:T(8,128)(2,1)S(1)}, u32[]{:S(2)}, u32[]{:S(2)}) collective-permute-start(bf16[512,256]{1,0:T(8,128)(2,1)} %get-tuple-element.12), channel_id=1, source_target_pairs={{1,2},{3,4},{5,6},{7,8},{9,10},{11,12},{13,14},{2,1},{4,3},{6,5},{... | collective-permute-start | bytes 786440 | tf_op jit(solution)/shard_map/ppermute | solution.py:458
  104.4 0.0 collective-permute-done.2.inner
  104.4 0.0 copy-start.2
  104.4 7.3 %collective-permute-done.3.outer = bf16[512,256]{1,0:T(8,128)(2,1)S(1)} collective-permute-done((bf16[512,256]{1,0:T(8,128)(2,1)}, bf16[512,256]{1,0:T(8,128)(2,1)S(1)}, u32[]{:S(2)}, u32[]{:S(2)}) %collective-permute-start.3) | collective-permute-done | bytes 262176 | tf_op jit(solution)/shard_map/ppermute | solution.py:458
  111.7 0.0 copy-start.3
  111.7 0.0 copy-done.2
  111.7 0.7 copy-done.3
  112.5 21.8 %level2.1 = (bf16[2048,256]{1,0:T(8,128)(2,1)}, bf16[256,256]{1,0:T(8,128)(2,1)}, bf16[256,256]{1,0:T(8,128)(2,1)}) custom-call(s32[1]{0:T(128)} %bitcast.base_ref, s32[8,2048]{1,0:T(8,128)} %bitcast.8, s32[8,2048]{1,0:T(8,128)} %bitcast.9, f32[2560,256]{1,0:T(8,128)} %get-tuple-element.10.part, bf16[512,256]{1,0:T(8,128)(2,1)} %copy-done.2, ...), custom_call_target="tpu_custom_call" | custom-call | flops 4294967296 | bytes 2621440 | tf_op jit(solution)/shard_map/level2/pallas_call | solution.py:346
  134.3 0.1 collective-permute-start.4
  134.4 4.0 %collective-permute-start.5 = (bf16[256,256]{1,0:T(8,128)(2,1)}, bf16[256,256]{1,0:T(8,128)(2,1)S(1)}, u32[]{:S(2)}, u32[]{:S(2)}) collective-permute-start(bf16[256,256]{1,0:T(8,128)(2,1)} %get-tuple-element.15), channel_id=1, source_target_pairs={{1,2},{3,4},{5,6},{7,8},{9,10},{11,12},{13,14},{2,1},{4,3},{6,5},{... | collective-permute-start | bytes 393224 | tf_op jit(solution)/shard_map/ppermute | solution.py:458
  138.4 0.0 collective-permute-done.4.near
  138.4 0.0 copy-start.4
  138.4 6.1 %collective-permute-done.5.far = bf16[256,256]{1,0:T(8,128)(2,1)S(1)} collective-permute-done((bf16[256,256]{1,0:T(8,128)(2,1)}, bf16[256,256]{1,0:T(8,128)(2,1)S(1)}, u32[]{:S(2)}, u32[]{:S(2)}) %collective-permute-start.5) | collective-permute-done | bytes 131104 | tf_op jit(solution)/shard_map/ppermute | solution.py:458
  144.5 0.0 copy-start.5
  144.5 0.0 copy-done.4
  144.5 0.7 copy-done.5
  145.1 14.9 %down.1 = bf16[8192,256]{1,0:T(8,128)(2,1)} custom-call(s32[1]{0:T(128)} %bitcast.base_ref, s32[64,128]{1,0:T(8,128)} %bitcast.11, bf16[8192,256]{1,0:T(8,128)(2,1)} %get-tuple-element.9.h1a, bf16[2048,256]{1,0:T(8,128)(2,1)} %get-tuple-element.8.h2o, bf16[256,256]{1,0:T(8,128)(2,1)} %copy-done.4, bf16[256,256]{1,0:T(8,128)(2,1)} %copy-done.5, ...), custom_call_target="tpu_custom_call" | custom-call | flops 5368709120 | bytes 8388608 | tf_op jit(solution)/shard_map/down/pallas_call | solution.py:422
Async XLA Ops:
  3.2 15.5 %collective-permute-start.1 = (bf16[1280,256]{1,0:T(8,128)(2,1)S(1)}, bf16[1280,256]{1,0:T(8,128)(2,1)S(1)}, u32[]{:S(2)}, u32[]{:S(2)}) collective-permute-start(bf16[1280,256]{1,0:T(8,128)(2,1)S(1)} %get-tuple-element.18), channel_id=1, source_target_pairs={{1,2},{3,4},{5,6},{7,8},{9,10},{11,12},{13,14},{15,16},{17,18},{19... | collective-permute-start | bytes 1966088 | tf_op jit(solution)/shard_map/ppermute | solution.py:458
  7.2 11.5 %collective-permute-start = (bf16[1280,256]{1,0:T(8,128)(2,1)S(1)}, bf16[1280,256]{1,0:T(8,128)(2,1)S(1)}, u32[]{:S(2)}, u32[]{:S(2)}) collective-permute-start(bf16[1280,256]{1,0:T(8,128)(2,1)S(1)} %get-tuple-element.19), channel_id=1, source_target_pairs={{0,1},{2,3},{4,5},{6,7},{8,9},{10,11},{12,13},{14,15},{16,17},{18,... | collective-permute-start | bytes 1966088 | tf_op jit(solution)/shard_map/ppermute | solution.py:458
  18.7 0.8 copy-start
  18.7 1.1 copy-start.1
  100.1 4.3 %collective-permute-start.2 = (bf16[512,256]{1,0:T(8,128)(2,1)}, bf16[512,256]{1,0:T(8,128)(2,1)S(1)}, u32[]{:S(2)}, u32[]{:S(2)}) collective-permute-start(bf16[512,256]{1,0:T(8,128)(2,1)} %get-tuple-element.11), channel_id=1, source_target_pairs={{0,1},{2,3},{4,5},{6,7},{8,9},{10,11},{12,13},{14,15},{1,0},{3,2},... | collective-permute-start | bytes 786440 | tf_op jit(solution)/shard_map/ppermute | solution.py:458
  100.2 11.5 %collective-permute-start.3 = (bf16[512,256]{1,0:T(8,128)(2,1)}, bf16[512,256]{1,0:T(8,128)(2,1)S(1)}, u32[]{:S(2)}, u32[]{:S(2)}) collective-permute-start(bf16[512,256]{1,0:T(8,128)(2,1)} %get-tuple-element.12), channel_id=1, source_target_pairs={{1,2},{3,4},{5,6},{7,8},{9,10},{11,12},{13,14},{2,1},{4,3},{6,5},{... | collective-permute-start | bytes 786440 | tf_op jit(solution)/shard_map/ppermute | solution.py:458
  104.4 7.3 %copy-start.2 = (bf16[512,256]{1,0:T(8,128)(2,1)}, bf16[512,256]{1,0:T(8,128)(2,1)S(1)}, u32[]{:S(2)}) copy-start(bf16[512,256]{1,0:T(8,128)(2,1)S(1)} %collective-permute-done.2.inner) | copy-start | bytes 786436
  111.7 0.7 copy-start.3
  134.3 4.1 %collective-permute-start.4 = (bf16[256,256]{1,0:T(8,128)(2,1)}, bf16[256,256]{1,0:T(8,128)(2,1)S(1)}, u32[]{:S(2)}, u32[]{:S(2)}) collective-permute-start(bf16[256,256]{1,0:T(8,128)(2,1)} %get-tuple-element.14), channel_id=1, source_target_pairs={{0,1},{2,3},{4,5},{6,7},{8,9},{10,11},{12,13},{14,15},{1,0},{3,2},... | collective-permute-start | bytes 393224 | tf_op jit(solution)/shard_map/ppermute | solution.py:458
  134.4 10.1 %collective-permute-start.5 = (bf16[256,256]{1,0:T(8,128)(2,1)}, bf16[256,256]{1,0:T(8,128)(2,1)S(1)}, u32[]{:S(2)}, u32[]{:S(2)}) collective-permute-start(bf16[256,256]{1,0:T(8,128)(2,1)} %get-tuple-element.15), channel_id=1, source_target_pairs={{1,2},{3,4},{5,6},{7,8},{9,10},{11,12},{13,14},{2,1},{4,3},{6,5},{... | collective-permute-start | bytes 393224 | tf_op jit(solution)/shard_map/ppermute | solution.py:458
  138.4 6.1 %copy-start.4 = (bf16[256,256]{1,0:T(8,128)(2,1)}, bf16[256,256]{1,0:T(8,128)(2,1)S(1)}, u32[]{:S(2)}) copy-start(bf16[256,256]{1,0:T(8,128)(2,1)S(1)} %collective-permute-done.4.near) | copy-start | bytes 393220
  144.5 0.7 copy-start.5
